TPU v7x, 32 devices: a whole 2x2x4 slice. The times are simulated.
32 devices in a mesh: aa: 4 (over z), ba: 2 (over core), col: 4 (over y, x).
Axes of the slice: x: 2, y: 2, z: 4, core: 2. Of those that a mesh axis runs over, the one named last changes fastest.
Arguments:
- density: float32 [128, 64, 512], P('aa', 'ba', 'col'), may hold values from 0.1 to 2
- lower_coupling: float32 [128, 64, 512], P('aa', 'ba', 'col'), may hold values from 0.005 to 40000
- upper_coupling: float32 [128, 64, 512], P('aa', 'ba', 'col'), may hold values from 0.005 to 40000
- reaction: float32 [128, 64, 512], P('aa', 'ba', 'col'), may hold values from 0.5 to 2
- cross_weight: float32 [128, 64, 512], P('aa', 'ba', 'col'), may hold values from -1 to 1
Outputs:
- new_density: float32 [128, 64, 512], P('aa', 'ba', 'col')
All inputs are finite; a program needn't handle non-finite values.
Results may differ from a plain program's by a relative error of at most 0.0019.
Values sent between devices are 32-bit elements; how exact they have to be, the bound alone decides.
A program may use at most 64 MiB of HBM per device.

v0:
```python
import functools

import jax
import jax.numpy as jnp
from jax import lax
from jax.experimental import pallas as pl
from jax.experimental.pallas import tpu as pltpu
from jax.sharding import PartitionSpec as P

MESH = pl.DeviceIdType.MESH
SUB, LANES = 8, 128


def kernel(
    line, cols, p_hbm, l_hbm, u_hbm, s_hbm, w_hbm, x_hbm,
    p, l, u, s, w, x, t, r, f, o, b,
    edge_out, edge_in, row_out, row_in, mat_out, mat_in, rhs_out, rhs_in, res_out, res_in,
    load_sem, store_sem, edge_send, edge_recv, row_send, row_recv,
    mat_send, mat_recv, rhs_send, rhs_recv, res_send, res_recv,
):
    rows, width, _ = p.shape
    half = rows // 2
    tiles = width // SUB
    aa, ba, col = lax.axis_index("aa"), lax.axis_index("ba"), lax.axis_index("col")
    other = 1 - ba
    left, right = lax.rem(col + cols - 1, cols), lax.rem(col + 1, cols)

    loads = [
        pltpu.make_async_copy(src, dst, load_sem.at[i])
        for i, (src, dst) in enumerate(((p_hbm, p), (l_hbm, l), (u_hbm, u), (s_hbm, s), (w_hbm, w)))
    ]
    for load in loads:
        load.start()

    barrier = pltpu.get_barrier_semaphore()
    beside = [(aa, other, col)] + [(aa, half_b, c) for c in (left, right) for half_b in (ba, other)]
    along = [(lax.rem(aa + d, line), ba, col) for d in range(1, line)]
    for device in beside + along:
        pl.semaphore_signal(barrier, inc=1, device_id=device, device_id_type=MESH)

    def send(src, dst, send_sem, recv_sem, device):
        return pltpu.make_async_remote_copy(
            src_ref=src, dst_ref=dst, send_sem=send_sem, recv_sem=recv_sem,
            device_id=device, device_id_type=MESH,
        )

    lane = lax.broadcasted_iota(jnp.int32, (SUB, LANES), 1)
    sub = lax.broadcasted_iota(jnp.int32, (SUB, LANES), 0)
    plane_lane = lax.broadcasted_iota(jnp.int32, (width, LANES), 1)
    plane_sub = lax.broadcasted_iota(jnp.int32, (width, LANES), 0)
    lower_half = (ba == 0).astype(jnp.float32)
    upper_half = 1.0 - lower_half

    loads[0].wait()
    parts = []
    for k in range(tiles):
        last = jnp.zeros((SUB, LANES), jnp.float32)
        first = last
        for a in range(rows):
            j = k * rows + a
            moved = pltpu.roll(p[a, k * SUB : (k + 1) * SUB, :], (j + 1) % LANES, 1)
            last = jnp.where(lane == j, moved, last)
            first = jnp.where(lane == (j + 1) % LANES, moved, first)
        parts.append((last, first))
    last = functools.reduce(jnp.add, [part[0] for part in parts])
    first = functools.reduce(jnp.add, [part[1] for part in parts])
    edge_out[0] = last
    edge_out[1] = pltpu.roll(first, LANES - 1, 1)
    row_out[...] = jnp.where(ba == 0, p[:, width - 1, :], p[:, 0, :])

    pl.semaphore_wait(barrier, len(beside) + len(along))

    halo = [send(row_out, row_in, row_send, row_recv, (aa, other, col))]
    for side, target in ((0, right), (1, left)):
        for which, half_b in ((0, ba), (1, other)):
            i = 2 * side + which
            halo.append(
                send(edge_out.at[side], edge_in.at[i], edge_send.at[i], edge_recv.at[i], (aa, half_b, target))
            )
    for copy in halo:
        copy.start()

    for load in loads[1:4]:
        load.wait()
    ends = []
    for order, outer, inner in (
        (tuple(range(half)), l, u),
        (tuple(range(rows - 1, half - 1, -1)), u, l),
    ):
        ends.append([order, outer, inner, None, None, None, None])
    for i in range(half):
        for end in ends:
            order, outer, inner, keep, fill, far, run = end
            a = order[i]
            excess = s[a] + (outer[a] if keep is None else outer[a] * keep)
            scale = 1.0 / (excess + inner[a])
            ratio = inner[a] * scale
            weight = outer[a] * scale
            keep = excess * scale
            fill = weight if fill is None else weight * fill
            t[a], r[a], f[a] = scale, ratio, fill
            far = fill if far is None else far + run * fill
            run = ratio if run is None else run * ratio
            end[3:] = [keep, fill, far, run]
    (keep1, f1, far1, run1), (keep2, f2, far2, run2) = ends[0][3:], ends[1][3:]
    r1, r2 = r[half - 1], r[half]
    joint = 1.0 / (keep1 + r1 * keep2)
    link1, link2 = run1 * joint, run2 * joint
    spikes = (far1 + link1 * (r2 * f1), link1 * f2, link2 * f1, far2 + link2 * (r1 * f2))
    for i, spike in enumerate(spikes):
        for k in range(tiles):
            mat_out[k, i] = spike[k * SUB : (k + 1) * SUB]

    stride = line // tiles
    mine = aa // stride
    solves = None if stride == 1 else lax.rem(aa, stride) == 0

    def solver_only(body):
        if solves is None:
            body()
        else:
            pl.when(solves)(body)

    def to_solvers(out, into, send_sem, recv_sem, act):
        def one(d):
            k = lax.rem(mine + d, tiles)
            act(send(out.at[k], into.at[aa], send_sem.at[k], recv_sem.at[aa], (k * stride, ba, col)))

        for d in range(1, tiles):
            one(d)
        if solves is not None:
            pl.when(jnp.logical_not(solves))(lambda: one(0))

    def from_line(into, send_sem, recv_sem):
        for d in range(1, line):
            j = lax.rem(aa + d, line)
            send(into.at[j], into.at[j], send_sem.at[0], recv_sem.at[j], (j, ba, col)).wait_recv()

    to_solvers(mat_out, mat_in, mat_send, mat_recv, lambda copy: copy.start())

    loads[4].wait()

    def across(value, lanes):
        after = jnp.where(lanes < LANES - 1, pltpu.roll(value, LANES - 1, 1), 0.0)
        return after - jnp.where(lanes > 0, pltpu.roll(value, 1, 1), 0.0)

    for a in range(rows):
        value = p[a]
        step = across(value, plane_lane)
        mixed = jnp.where(plane_sub < width - 1, pltpu.roll(step, width - 1, 0), 0.0)
        mixed = mixed - jnp.where(plane_sub > 0, pltpu.roll(step, 1, 0), 0.0)
        b[a] = value + w[a] * mixed

    for copy in halo:
        copy.wait_recv()

    def column(same, opposite):
        def up(value):
            return pltpu.roll(value, SUB - 1, 0)

        def down(value):
            return pltpu.roll(value, 1, 0)

        ahead = jnp.where(
            lane < LANES - rows,
            pltpu.roll(up(same), LANES - rows, 1),
            pltpu.roll(up(opposite), LANES - rows, 1) * lower_half,
        )
        behind = jnp.where(
            lane >= rows, pltpu.roll(down(same), rows, 1), pltpu.roll(down(opposite), rows, 1) * upper_half
        )
        return jnp.where(sub < SUB - 1, up(same), ahead) - jnp.where(sub > 0, down(same), behind)

    from_left = column(edge_in[0], edge_in[1]) * jnp.where(col > 0, -1.0, 0.0)
    from_right = column(edge_in[2], edge_in[3]) * jnp.where(col < cols - 1, 1.0, 0.0)
    from_left = pltpu.roll(from_left, 1, 1)
    odd = lax.rem(lane, 2) == 1
    pairs = (jnp.where(odd, from_left, from_right), jnp.where(odd, from_right, from_left))
    at_edge = jnp.logical_or(lane == 0, lane == LANES - 1)
    row_step = across(row_in[...], lax.broadcasted_iota(jnp.int32, (rows, LANES), 1))
    row_in[...] = row_step * (lower_half - upper_half)

    def side(a):
        line_in = row_in[a : a + 1, :]
        terms = []
        for k in range(tiles):
            term = jnp.where(at_edge, pltpu.roll(pairs[a % 2], (LANES - 1 - k * rows - a) % LANES, 1), 0.0)
            if k == 0:
                term = term + jnp.where(sub == 0, line_in * upper_half, 0.0)
            if k == tiles - 1:
                term = term + jnp.where(sub == SUB - 1, line_in * lower_half, 0.0)
            terms.append(term)
        return b[a] + w[a] * jnp.concatenate(terms, axis=0)

    state = [[None, None, None], [None, None, None]]
    for i in range(half):
        for end, held in zip(ends, state):
            order, outer = end[0], end[1]
            a = order[i]
            offset, far, run = held
            offset = side(a) * t[a] if offset is None else (side(a) + outer[a] * offset) * t[a]
            o[a] = offset
            far = offset if far is None else far + run * offset
            run = r[a] if run is None else run * r[a]
            held[:] = [offset, far, run]
    (o1, far1, _), (o2, far2, _) = state
    for i, value in enumerate((far1 + link1 * (o2 + r2 * o1), far2 + link2 * (o1 + r1 * o2))):
        for k in range(tiles):
            rhs_out[k, i] = value[k * SUB : (k + 1) * SUB]
    to_solvers(rhs_out, rhs_in, rhs_send, rhs_recv, lambda copy: copy.start())

    def reduced():
        mat_in[aa] = mat_out[mine]
        rhs_in[aa] = rhs_out[mine]
        from_line(mat_in, mat_send, mat_recv)
        slope = []
        before = jnp.zeros((SUB, LANES), jnp.float32)
        for j in range(line):
            first_l, first_r, last_l, last_r = (mat_in[j, i] for i in range(4))
            inverse = 1.0 / (1.0 - first_l * before)
            slope.append((before, inverse, inverse * first_r, first_l, last_l))
            before = last_r + last_l * before * slope[j][2]
        from_line(rhs_in, rhs_send, rhs_recv)
        base = []
        shift = jnp.zeros((SUB, LANES), jnp.float32)
        for j in range(line):
            before, inverse, _, first_l, last_l = slope[j]
            start = inverse * (rhs_in[j, 0] + first_l * shift)
            base.append((shift, start))
            shift = rhs_in[j, 1] + last_l * (shift + before * start)
        after = jnp.zeros((SUB, LANES), jnp.float32)
        for j in range(line - 1, -1, -1):
            res_out[j, 1] = after
            after = base[j][1] + slope[j][2] * after
            res_out[j, 0] = base[j][0] + slope[j][0] * after
        for d in range(1, line):
            j = lax.rem(aa + d, line)
            send(res_out.at[j], res_in.at[mine], res_send.at[j], res_recv.at[mine], (j, ba, col)).start()
        res_in[mine] = res_out[aa]

    solver_only(reduced)

    def from_solver(d):
        k = lax.rem(mine + d, tiles)
        send(
            res_in.at[k], res_in.at[k], res_send.at[0], res_recv.at[k], (k * stride, ba, col)
        ).wait_recv()

    for d in range(1, tiles):
        from_solver(d)
    if solves is not None:
        pl.when(jnp.logical_not(solves))(lambda: from_solver(0))

    before = jnp.concatenate([res_in[k, 0] for k in range(tiles)], axis=0)
    after = jnp.concatenate([res_in[k, 1] for k in range(tiles)], axis=0)
    top, bottom = o[half - 1] + f[half - 1] * before, o[half] + f[half] * after
    upper, lower = joint * (top + r1 * bottom), joint * (bottom + r2 * top)
    x[half - 1], x[half] = upper, lower
    for i in range(1, half):
        a, c = half - 1 - i, half + i
        upper = (o[a] + f[a] * before) + r[a] * upper
        lower = (o[c] + f[c] * after) + r[c] * lower
        x[a], x[c] = upper, lower
    store = pltpu.make_async_copy(x, x_hbm, store_sem)
    store.start()

    for copy in halo:
        copy.wait_send()
    to_solvers(mat_out, mat_in, mat_send, mat_recv, lambda copy: copy.wait_send())
    to_solvers(rhs_out, rhs_in, rhs_send, rhs_recv, lambda copy: copy.wait_send())

    def results_sent():
        for d in range(1, line):
            j = lax.rem(aa + d, line)
            send(
                res_out.at[j], res_in.at[mine], res_send.at[j], res_recv.at[mine], (j, ba, col)
            ).wait_send()

    solver_only(results_sent)
    store.wait()


def shards(line, cols, density, lower_coupling, upper_coupling, reaction, cross_weight):
    rows, width, lanes = density.shape
    tiles = width // SUB
    assert lanes == LANES and rows * tiles == LANES and line % tiles == 0
    block = pltpu.VMEM((rows, width, lanes), jnp.float32)

    def tile(*lead):
        return pltpu.VMEM((*lead, SUB, LANES), jnp.float32)

    dma = pltpu.SemaphoreType.DMA
    return pl.pallas_call(
        functools.partial(kernel, line, cols),
        out_shape=jax.ShapeDtypeStruct(density.shape, jnp.float32),
        in_specs=[pl.BlockSpec(memory_space=pl.ANY)] * 5,
        out_specs=pl.BlockSpec(memory_space=pl.ANY),
        scratch_shapes=[block] * 11
        + [
            tile(2),
            tile(4),
            pltpu.VMEM((rows, lanes), jnp.float32),
            pltpu.VMEM((rows, lanes), jnp.float32),
            tile(tiles, 4),
            tile(line, 4),
            tile(tiles, 2),
            tile(line, 2),
            tile(line, 2),
            tile(tiles, 2),
            dma((5,)),
            dma,
            dma((4,)),
            dma((4,)),
            dma,
            dma,
            dma((tiles,)),
            dma((line,)),
            dma((tiles,)),
            dma((line,)),
            dma((line,)),
            dma((tiles,)),
        ],
        compiler_params=pltpu.CompilerParams(
            collective_id=0, has_side_effects=True, vmem_limit_bytes=32 * 1024 * 1024
        ),
    )(density, lower_coupling, upper_coupling, reaction, cross_weight)


def solution(mesh):
    spec = P("aa", "ba", "col")
    body = functools.partial(shards, mesh.shape["aa"], mesh.shape["col"])
    return jax.shard_map(body, mesh=mesh, in_specs=(spec,) * 5, out_specs=spec, check_vma=False)
```

profile of v0, /device:TPU:0, one launch (start us, length us, event | category | flops | bytes accessed | tf_op | source)
XLA Modules:
  0.0 23.5 jit_solution(4775813549882680124)
XLA Ops:
  0.0 0.0 copy-start
  0.0 1.0 %copy-done = f32[32,32,128]{2,1,0:T(8,128)S(1)} copy-done((f32[32,32,128]{2,1,0:T(8,128)S(1)}, f32[32,32,128]{2,1,0:T(8,128)}, u32[]{:S(2)}) %copy-start) | copy-done | bytes 524312
  1.0 0.0 copy-start.1
  1.0 1.0 %copy-done.1 = f32[32,32,128]{2,1,0:T(8,128)S(1)} copy-done((f32[32,32,128]{2,1,0:T(8,128)S(1)}, f32[32,32,128]{2,1,0:T(8,128)}, u32[]{:S(2)}) %copy-start.1) | copy-done | bytes 524312
  2.1 0.0 copy-start.2
  2.1 1.0 %copy-done.2 = f32[32,32,128]{2,1,0:T(8,128)S(1)} copy-done((f32[32,32,128]{2,1,0:T(8,128)S(1)}, f32[32,32,128]{2,1,0:T(8,128)}, u32[]{:S(2)}) %copy-start.2) | copy-done | bytes 524312
  3.1 0.0 copy-start.3
  3.1 1.0 %copy-done.3 = f32[32,32,128]{2,1,0:T(8,128)S(1)} copy-done((f32[32,32,128]{2,1,0:T(8,128)S(1)}, f32[32,32,128]{2,1,0:T(8,128)}, u32[]{:S(2)}) %copy-start.3) | copy-done | bytes 524312
  4.2 0.0 copy-start.4
  4.2 1.0 %copy-done.4 = f32[32,32,128]{2,1,0:T(8,128)S(1)} copy-done((f32[32,32,128]{2,1,0:T(8,128)S(1)}, f32[32,32,128]{2,1,0:T(8,128)}, u32[]{:S(2)}) %copy-start.4) | copy-done | bytes 524312
  5.2 17.4 %shard_map.55 = f32[32,32,128]{2,1,0:T(8,128)S(1)} custom-call(f32[32,32,128]{2,1,0:T(8,128)S(1)} %copy-done, f32[32,32,128]{2,1,0:T(8,128)S(1)} %copy-done.1, f32[32,32,128]{2,1,0:T(8,128)S(1)} %copy-done.2, f32[32,32,128]{2,1,0:T(8,128)S(1)} %copy-done.3, f32[32,32,128]{2,1,0:T(8,128)S(1)} %copy-done.4), custom_call_target="tpu_custom_call" | custom-call | tf_op jit(solution)/shard_map/pallas_call | solution.py:293
  22.7 0.8 %copy.7 = f32[32,32,128]{2,1,0:T(8,128)} copy(f32[32,32,128]{2,1,0:T(8,128)S(1)} %shard_map.55) | data formatting | bytes 1048576
Async XLA Ops:
  0.0 1.0 %copy-start = (f32[32,32,128]{2,1,0:T(8,128)S(1)}, f32[32,32,128]{2,1,0:T(8,128)}, u32[]{:S(2)}) copy-start(f32[32,32,128]{2,1,0:T(8,128)} %p_hbm.1) | copy-start | bytes 1572868
  1.0 1.0 %copy-start.1 = (f32[32,32,128]{2,1,0:T(8,128)S(1)}, f32[32,32,128]{2,1,0:T(8,128)}, u32[]{:S(2)}) copy-start(f32[32,32,128]{2,1,0:T(8,128)} %l_hbm.1) | copy-start | bytes 1572868
  2.1 1.0 %copy-start.2 = (f32[32,32,128]{2,1,0:T(8,128)S(1)}, f32[32,32,128]{2,1,0:T(8,128)}, u32[]{:S(2)}) copy-start(f32[32,32,128]{2,1,0:T(8,128)} %u_hbm.1) | copy-start | bytes 1572868
  3.1 1.0 %copy-start.3 = (f32[32,32,128]{2,1,0:T(8,128)S(1)}, f32[32,32,128]{2,1,0:T(8,128)}, u32[]{:S(2)}) copy-start(f32[32,32,128]{2,1,0:T(8,128)} %s_hbm.1) | copy-start | bytes 1572868
  4.2 1.0 %copy-start.4 = (f32[32,32,128]{2,1,0:T(8,128)S(1)}, f32[32,32,128]{2,1,0:T(8,128)}, u32[]{:S(2)}) copy-start(f32[32,32,128]{2,1,0:T(8,128)} %w_hbm.1) | copy-start | bytes 1572868
where the time goes:
time: 23.8 us; the launch traced here: 23.5 us
  Pallas kernels  17.4 us (73%)
  local copies, waits for them, and re-layouts  6 us (25%)
    pallas_call x1, Pallas kernels, shards(): pl.pallas_call(functools.partial(kernel, line, cols), out_shape=jax.Shape...  17.4 us
    unnamed x11, local copies, waits for them, and re-layouts  6 us

commit v1 on v0

--- a/solution.py
+++ b/solution.py
@@ -12,10 +12,10 @@
 
 
 def kernel(
-    line, cols, p_hbm, l_hbm, u_hbm, s_hbm, w_hbm, x_hbm,
-    p, l, u, s, w, x, t, r, f, o, b,
+    line, cols, p_hbm, l_hbm, u_hbm, s_hbm, w_hbm, x,
+    p, l, u, s, w, t, r, f, o, b,
     edge_out, edge_in, row_out, row_in, mat_out, mat_in, rhs_out, rhs_in, res_out, res_in,
-    load_sem, store_sem, edge_send, edge_recv, row_send, row_recv,
+    load_sem, edge_send, edge_recv, row_send, row_recv,
     mat_send, mat_recv, rhs_send, rhs_recv, res_send, res_recv,
 ):
     rows, width, _ = p.shape
@@ -261,8 +261,6 @@
         upper = (o[a] + f[a] * before) + r[a] * upper
         lower = (o[c] + f[c] * after) + r[c] * lower
         x[a], x[c] = upper, lower
-    store = pltpu.make_async_copy(x, x_hbm, store_sem)
-    store.start()
 
     for copy in halo:
         copy.wait_send()
@@ -277,7 +275,6 @@
             ).wait_send()
 
     solver_only(results_sent)
-    store.wait()
 
 
 def shards(line, cols, density, lower_coupling, upper_coupling, reaction, cross_weight):
@@ -292,10 +289,10 @@
     dma = pltpu.SemaphoreType.DMA
     return pl.pallas_call(
         functools.partial(kernel, line, cols),
-        out_shape=jax.ShapeDtypeStruct(density.shape, jnp.float32),
+        out_shape=pltpu.VMEM(density.shape, jnp.float32),
         in_specs=[pl.BlockSpec(memory_space=pl.ANY)] * 5,
-        out_specs=pl.BlockSpec(memory_space=pl.ANY),
-        scratch_shapes=[block] * 11
+        out_specs=pl.BlockSpec(memory_space=pltpu.VMEM),
+        scratch_shapes=[block] * 10
         + [
             tile(2),
             tile(4),
@@ -308,7 +305,6 @@
             tile(line, 2),
             tile(tiles, 2),
             dma((5,)),
-            dma,
             dma((4,)),
             dma((4,)),
             dma,
@@ -321,7 +317,7 @@
             dma((tiles,)),
         ],
         compiler_params=pltpu.CompilerParams(
-            collective_id=0, has_side_effects=True, vmem_limit_bytes=32 * 1024 * 1024
+            collective_id=0, has_side_effects=True, vmem_limit_bytes=55 * 1024 * 1024
         ),
     )(density, lower_coupling, upper_coupling, reaction, cross_weight)
 

time: 23.8 us -> 18.1 us (0.76)
  local copies, waits for them, and re-layouts: 6 us -> 0.8 us
    unnamed x11 -> x1, local copies, waits for them, and re-layouts: 6 us -> 0.8 us
    pallas_call x1, Pallas kernels: 17.4 us -> 17.2 us  [shards(): pl.pallas_call(functools.partial(kernel, line, cols), out_shape=pltpu.VME...]
where the time goes in v1:
time: 18.1 us; the launch traced here: 18 us
  Pallas kernels  17.2 us (95%)
  local copies, waits for them, and re-layouts  0.8 us (4%)
    pallas_call x1, Pallas kernels, shards(): pl.pallas_call(functools.partial(kernel, line, cols), out_shape=pltpu.VME...  17.2 us
    unnamed x1, local copies, waits for them, and re-layouts  0.8 us

profile of v1, /device:TPU:0, one launch (start us, length us, event | category | flops | bytes accessed | tf_op | source)
XLA Modules:
  0.0 18.0 jit_solution(7845799225522185635)
XLA Ops:
  0.0 17.2 %shard_map.55 = f32[32,32,128]{2,1,0:T(8,128)S(1)} custom-call(f32[32,32,128]{2,1,0:T(8,128)} %p_hbm.1, f32[32,32,128]{2,1,0:T(8,128)} %l_hbm.1, f32[32,32,128]{2,1,0:T(8,128)} %u_hbm.1, f32[32,32,128]{2,1,0:T(8,128)} %s_hbm.1, f32[32,32,128]{2,1,0:T(8,128)} %w_hbm.1), custom_call_target="tpu_custom_call" | custom-call | tf_op jit(solution)/shard_map/pallas_call | solution.py:290
  17.2 0.8 %copy.7 = f32[32,32,128]{2,1,0:T(8,128)} copy(f32[32,32,128]{2,1,0:T(8,128)S(1)} %shard_map.55) | data formatting | bytes 1048576

commit v2 on v1

--- a/solution.py
+++ b/solution.py
@@ -99,6 +99,7 @@
             keep = excess * scale
             fill = weight if fill is None else weight * fill
             t[a], r[a], f[a] = scale, ratio, fill
+            outer[a] = weight
             far = fill if far is None else far + run * fill
             run = ratio if run is None else run * ratio
             end[3:] = [keep, fill, far, run]
@@ -149,7 +150,8 @@
         step = across(value, plane_lane)
         mixed = jnp.where(plane_sub < width - 1, pltpu.roll(step, width - 1, 0), 0.0)
         mixed = mixed - jnp.where(plane_sub > 0, pltpu.roll(step, 1, 0), 0.0)
-        b[a] = value + w[a] * mixed
+        b[a] = (value + w[a] * mixed) * t[a]
+        w[a] = w[a] * t[a]
 
     for copy in halo:
         copy.wait_recv()
@@ -198,7 +200,7 @@
             order, outer = end[0], end[1]
             a = order[i]
             offset, far, run = held
-            offset = side(a) * t[a] if offset is None else (side(a) + outer[a] * offset) * t[a]
+            offset = side(a) if offset is None else side(a) + outer[a] * offset
             o[a] = offset
             far = offset if far is None else far + run * offset
             run = r[a] if run is None else run * r[a]

time: 18.1 us -> 18.1 us (level)
  no operation moved by 1% of the time
where the time goes in v2:
time: 18.1 us; the launch traced here: 18 us
  Pallas kernels  17.2 us (95%)
  local copies, waits for them, and re-layouts  0.8 us (4%)
    pallas_call x1, Pallas kernels, shards(): pl.pallas_call(functools.partial(kernel, line, cols), out_shape=pltpu.VME...  17.2 us
    unnamed x1, local copies, waits for them, and re-layouts  0.8 us

profile of v2, /device:TPU:0, one launch (start us, length us, event | category | flops | bytes accessed | tf_op | source)
XLA Modules:
  0.0 18.0 jit_solution(15767660229601302138)
XLA Ops:
  0.0 17.2 %shard_map.55 = f32[32,32,128]{2,1,0:T(8,128)S(1)} custom-call(f32[32,32,128]{2,1,0:T(8,128)} %p_hbm.1, f32[32,32,128]{2,1,0:T(8,128)} %l_hbm.1, f32[32,32,128]{2,1,0:T(8,128)} %u_hbm.1, f32[32,32,128]{2,1,0:T(8,128)} %s_hbm.1, f32[32,32,128]{2,1,0:T(8,128)} %w_hbm.1), custom_call_target="tpu_custom_call" | custom-call | tf_op jit(solution)/shard_map/pallas_call | solution.py:292
  17.2 0.8 %copy.7 = f32[32,32,128]{2,1,0:T(8,128)} copy(f32[32,32,128]{2,1,0:T(8,128)S(1)} %shard_map.55) | data formatting | bytes 1048576
